TPU v7x, 512 devices: a whole 4x8x8 slice. The times are simulated.
512 devices in a mesh: store: 64 (over y, x, core), mp: 8 (over z).
Axes of the slice: x: 4, y: 8, z: 8, core: 2. Of those that a mesh axis runs over, the one named last changes fastest.
Arguments:
- queries: bfloat16 [32768, 8192], P(('store', 'mp')), may hold values from -6 to 6
- question_keys: bfloat16 [32768, 1024], P(('store', 'mp')), may hold values from -6 to 6
- question_values: bfloat16 [32768, 1024], P(('store', 'mp')), may hold values from -6 to 6
- stored_keys: bfloat16 [512, 128, 1024], P('store', None, 'mp'), may hold values from -6 to 6
- stored_values: bfloat16 [512, 128, 1024], P('store', None, 'mp'), may hold values from -6 to 6
- storage_row: int32 [512], replicated, may hold values from 0 to 511, as said below
- retrieved: int32 [256, 16], P('store'), may hold values from 0 to 511, as said below
Outputs:
- attended: bfloat16 [32768, 8192], P(('store', 'mp'))
Inputs may be any that keep to these rules, and one draw needn't show every extreme that they name: storage_row is a permutation; the block at storage row p is held by store index p // 8. `retrieved`: the 4 requests s * 4 to s * 4 + 3 together retrieve 64 blocks held by 64 different store indices, one block from each.
All inputs are finite; a program needn't handle non-finite values.
Results may differ from a plain program's by a relative error of at most 0.009.
Values may be sent and summed in bfloat16 or wider, within the bound.
A program may use at most 64 MiB of HBM per device.

v0:
```python
import math
import jax
import jax.numpy as jnp
from jax import lax
from jax.sharding import PartitionSpec as P

HEAD_SIZE = 128
HEAD_GROUP = 8
REQUEST_TOKENS = 128


def near_part(query_rows, nearby_keys, token_count):
    scale = 1.0 / math.sqrt(HEAD_SIZE)
    near_scores = jnp.dot(query_rows, nearby_keys.T, preferred_element_type=jnp.float32) * scale
    row_token = jnp.arange(token_count * HEAD_GROUP) // HEAD_GROUP
    causal = jnp.arange(token_count)[None, :] <= row_token[:, None]
    return (jnp.where(causal, near_scores, -jnp.inf), causal)


def attend_head(
    query_rows, nearby_keys, nearby_values, remote_keys, remote_values, token_count, order
):
    scale = 1.0 / math.sqrt(HEAD_SIZE)
    near_scores, causal = near_part(query_rows, nearby_keys, token_count)
    start_max = jnp.max(near_scores, axis=1)
    near_weights = jnp.where(causal, jnp.exp(near_scores - start_max[:, None]), 0.0)
    start_total = jnp.sum(near_weights, axis=1)
    start_sum = jnp.dot(
        near_weights.astype(jnp.bfloat16), nearby_values, preferred_element_type=jnp.float32
    )

    def absorb(carry, holder):
        running_max, running_total, running_sum = carry
        block_keys = remote_keys[holder]
        block_values = remote_values[holder]
        scores = jnp.dot(query_rows, block_keys.T, preferred_element_type=jnp.float32) * scale
        new_max = jnp.maximum(running_max, jnp.max(scores, axis=1))
        shrink = jnp.exp(running_max - new_max)
        weights = jnp.exp(scores - new_max[:, None])
        new_total = running_total * shrink + jnp.sum(weights, axis=1)
        new_sum = running_sum * shrink[:, None] + jnp.dot(
            weights.astype(jnp.bfloat16), block_values, preferred_element_type=jnp.float32
        )
        return ((new_max, new_total, new_sum), None)

    final, unused = lax.scan(absorb, (start_max, start_total, start_sum), order)
    return (
        (final[2] / final[1][:, None])
        .astype(jnp.bfloat16)
        .reshape(token_count, HEAD_GROUP * HEAD_SIZE)
    )


def local(
    queries, question_keys, question_values, stored_keys, stored_values, storage_row, retrieved
):
    query_part, key_part, value_part = (
        lax.all_to_all(queries, "mp", split_axis=1, concat_axis=0, tiled=True),
        lax.all_to_all(question_keys, "mp", split_axis=1, concat_axis=0, tiled=True),
        lax.all_to_all(question_values, "mp", split_axis=1, concat_axis=0, tiled=True),
    )
    held = stored_keys.shape[0]
    own_index = lax.axis_index("store")
    store_count = lax.axis_size("store")
    request_count = retrieved.shape[0]
    topc_count = retrieved.shape[1]
    rows_mine = storage_row[retrieved.reshape(-1)]
    owner_mine = rows_mine // held
    all_lists = lax.all_gather(retrieved, "store", axis=0, tiled=True)
    all_rows = storage_row[all_lists.reshape(store_count, request_count * topc_count)]
    matched = all_rows // held == own_index
    wanted = jnp.sum(jnp.where(matched, all_rows % held + 1, 0), axis=1) - 1
    picked = jnp.maximum(wanted, 0)
    send_keys = stored_keys[picked]
    send_values = stored_values[picked]
    owner_table = owner_mine.reshape(request_count, topc_count)
    token_count = REQUEST_TOKENS
    width = HEAD_GROUP * HEAD_SIZE
    blocks = []
    fetched_keys, fetched_values = (
        lax.all_to_all(send_keys, "store", split_axis=0, concat_axis=0, tiled=True),
        lax.all_to_all(send_values, "store", split_axis=0, concat_axis=0, tiled=True),
    )
    for request in range(request_count):
        lower = request * token_count
        upper = lower + token_count
        query_rows = query_part[lower:upper, 0:width].reshape(token_count * HEAD_GROUP, HEAD_SIZE)
        nearby_keys = key_part[lower:upper, 0:HEAD_SIZE]
        nearby_values = value_part[lower:upper, 0:HEAD_SIZE]
        query_rows, nearby_keys, nearby_values = (query_rows, nearby_keys, nearby_values)
        pieces = attend_head(
            query_rows,
            nearby_keys,
            nearby_values,
            fetched_keys,
            fetched_values,
            token_count,
            owner_table[request],
        )
        blocks.append(pieces)
    result = jnp.concatenate(blocks, axis=0)
    return lax.all_to_all(result, "mp", split_axis=0, concat_axis=1, tiled=True)


def solution(mesh):
    return jax.shard_map(
        local,
        mesh=mesh,
        in_specs=(
            P(("store", "mp"), None),
            P(("store", "mp"), None),
            P(("store", "mp"), None),
            P("store", None, "mp"),
            P("store", None, "mp"),
            P(),
            P("store", None),
        ),
        out_specs=P(("store", "mp"), None),
        check_vma=False,
    )
```

profile of v0, /device:TPU:8, one launch (start us, length us, event | category | flops | bytes accessed | tf_op | source)
XLA Modules:
  0.0 592.1 jit_solution(7433230943649113645)
XLA Ops:
  0.0 1.6 copy_bitcast_fusion.2
  1.6 10.3 %all-to-all-start.1 = ((bf16[64,8,128]{2,0,1:T(8,128)(2,1)}), bf16[64,8,128]{2,0,1:T(8,128)(2,1)S(1)}, u32[]{:S(2)}, u32[]{:S(2)}) async-start(bf16[64,8,128]{2,0,1:T(8,128)(2,1)} %copy_bitcast_fusion.2), calls=%async_computation.1 | async-start | bytes 262144 | tf_op jit(solution)/shard_map/all_to_all | solution.py:59
  11.9 1.6 copy_bitcast_fusion.1
  13.5 7.5 %all-to-all-done.1 = bf16[64,8,128]{2,0,1:T(8,128)(2,1)S(1)} async-done(((bf16[64,8,128]{2,0,1:T(8,128)(2,1)}), bf16[64,8,128]{2,0,1:T(8,128)(2,1)S(1)}, u32[]{:S(2)}, u32[]{:S(2)}) %all-to-all-start.1) | async-done | bytes 131104 | tf_op jit(solution)/shard_map/all_to_all | solution.py:59
  21.0 3.4 all-to-all-start.2
  24.4 2.3 copy.42
  26.7 6.7 %all-to-all-done.2 = bf16[64,8,128]{2,0,1:T(8,128)(2,1)S(1)} async-done(((bf16[64,8,128]{2,0,1:T(8,128)(2,1)}), bf16[64,8,128]{2,0,1:T(8,128)(2,1)S(1)}, u32[]{:S(2)}, u32[]{:S(2)}) %all-to-all-start.2) | async-done | bytes 131104 | tf_op jit(solution)/shard_map/all_to_all | solution.py:60
  33.4 3.6 all-to-all-start
  37.0 49.8 %all-gather = s32[64,4,16]{2,1,0:T(4,128)S(1)} all-gather(s32[1,4,16]{2,1,0:T(4,128)S(1)} %bitcast.134), channel_id=1, replica_groups=mesh['store'=64,'mp'=8] {'store'}, dimensions={0}, use_global_device_ids=true | all-gather | bytes 16640 | tf_op jit(solution)/shard_map/all_gather | solution.py:69
  87.1 25.9 %gather_fusion.1 = s32[4096]{0:T(1024)S(1)} fusion(s32[512]{0:T(512)S(1)} %copy-done.1, s32[4096]{0:T(1024)S(1)} %broadcast_clamp_fusion), kind=kCustom, calls=%fused_computation.1 | custom fusion | bytes 49152 | tf_op jit(solution)/shard_map/gather | solution.py:70
  113.2 2.1 gather_fusion.3
  115.3 8.7 %all-to-all-start.4 = ((bf16[64,128,128]{2,1,0:T(8,128)(2,1)}), bf16[64,128,128]{2,1,0:T(8,128)(2,1)}, u32[]{:S(2)}, u32[]{:S(2)}) async-start(bf16[64,128,128]{2,1,0:T(8,128)(2,1)} %gather_fusion.3), calls=%async_computation.4 | async-start | bytes 4194304 | tf_op jit(solution)/shard_map/all_to_all | solution.py:82
  124.0 2.1 gather_fusion.2
  126.1 48.2 %all-to-all-done.4 = bf16[64,128,128]{2,1,0:T(8,128)(2,1)} async-done(((bf16[64,128,128]{2,1,0:T(8,128)(2,1)}), bf16[64,128,128]{2,1,0:T(8,128)(2,1)}, u32[]{:S(2)}, u32[]{:S(2)}) %all-to-all-start.4) | async-done | bytes 2097184 | tf_op jit(solution)/shard_map/all_to_all | solution.py:82
  174.3 6.5 %all-to-all-start.3 = ((bf16[64,128,128]{2,1,0:T(8,128)(2,1)}), bf16[64,128,128]{2,1,0:T(8,128)(2,1)}, u32[]{:S(2)}, u32[]{:S(2)}) async-start(bf16[64,128,128]{2,1,0:T(8,128)(2,1)} %gather_fusion.2), calls=%async_computation.3 | async-start | bytes 4194304 | tf_op jit(solution)/shard_map/all_to_all | solution.py:81
  186.8 44.3 %all-to-all-done.3 = bf16[64,128,128]{2,1,0:T(8,128)(2,1)} async-done(((bf16[64,128,128]{2,1,0:T(8,128)(2,1)}), bf16[64,128,128]{2,1,0:T(8,128)(2,1)}, u32[]{:S(2)}, u32[]{:S(2)}) %all-to-all-start.3) | async-done | bytes 2097184 | tf_op jit(solution)/shard_map/all_to_all | solution.py:81
  231.1 88.0 %while.59 = (s32[]{:T(128)}, f32[1024]{0:T(1024)S(1)}, f32[1024]{0:T(1024)S(1)}, f32[1024,128]{1,0:T(8,128)S(1)}, s32[16]{0:T(128)}, /*index=5*/bf16[64,128,128]...) while((s32[]{:T(128)}, f32[1024]{0:T(1024)S(1)}, ...), condition=%wide.region_24.25_spmd, body=%wide.region_21.24_spmd.sunk | while | flops 68159488 | bytes 3014827 | solution.py:46
  319.4 78.3 %while.58 = (s32[]{:T(128)}, f32[1024]{0:T(1024)S(1)}, f32[1024]{0:T(1024)S(1)}, f32[1024,128]{1,0:T(8,128)S(1)}, s32[16]{0:T(128)S(1)}, /*index=5*/bf16[64,128,...) while((s32[]{:T(128)}, f32[1024]{0:T(1024)S(1)}, ...), condition=%wide.region_18.19_spmd, body=%wide.region_15.18_spmd.sunk | while | flops 68159488 | bytes 3014827 | solution.py:46
  323.1 1.2 convolution_add_fusion.10
  328.0 1.2 convolution_add_fusion.10
  332.9 1.2 convolution_add_fusion.10
  337.8 1.2 convolution_add_fusion.10
  342.7 1.2 convolution_add_fusion.10
  347.6 1.2 convolution_add_fusion.10
  352.5 1.2 convolution_add_fusion.10
  357.3 1.2 convolution_add_fusion.10
  362.2 1.2 convolution_add_fusion.10
  367.1 1.2 convolution_add_fusion.10
  372.0 1.2 convolution_add_fusion.10
  376.9 1.2 convolution_add_fusion.10
  381.8 1.2 convolution_add_fusion.10
  386.7 1.2 convolution_add_fusion.10
  391.6 1.2 convolution_add_fusion.10
  396.5 1.2 convolution_add_fusion.10
  398.0 78.3 %while.57 = (s32[]{:T(128)}, f32[1024]{0:T(1024)S(1)}, f32[1024]{0:T(1024)S(1)}, f32[1024,128]{1,0:T(8,128)S(1)}, s32[16]{0:T(128)S(1)}, /*index=5*/bf16[64,128,...) while((s32[]{:T(128)}, f32[1024]{0:T(1024)S(1)}, ...), condition=%wide.region_12.13_spmd, body=%wide.region_9.12_spmd.sunk | while | flops 68159488 | bytes 3014827 | solution.py:46
  401.7 1.2 convolution_add_fusion.9
  406.6 1.2 convolution_add_fusion.9
  411.5 1.2 convolution_add_fusion.9
  416.4 1.2 convolution_add_fusion.9
  421.3 1.2 convolution_add_fusion.9
  426.2 1.2 convolution_add_fusion.9
  431.1 1.2 convolution_add_fusion.9
  436.0 1.2 convolution_add_fusion.9
  440.9 1.2 convolution_add_fusion.9
  445.8 1.2 convolution_add_fusion.9
  450.7 1.2 convolution_add_fusion.9
  455.5 1.2 convolution_add_fusion.9
  460.4 1.2 convolution_add_fusion.9
  465.3 1.2 convolution_add_fusion.9
  470.2 1.2 convolution_add_fusion.9
  475.1 1.2 convolution_add_fusion.9
  476.7 78.3 %while.56 = (s32[]{:T(128)}, f32[1024]{0:T(1024)S(1)}, f32[1024]{0:T(1024)S(1)}, f32[1024,128]{1,0:T(8,128)S(1)}, s32[16]{0:T(128)S(1)}, /*index=5*/bf16[64,128,...) while((s32[]{:T(128)}, f32[1024]{0:T(1024)S(1)}, ...), condition=%wide.region_6.7_spmd, body=%wide.region_3.6_spmd.sunk | while | flops 68159488 | bytes 3014827 | solution.py:46
  480.4 1.2 convolution_add_fusion.8
  485.2 1.2 convolution_add_fusion.8
  490.1 1.2 convolution_add_fusion.8
  495.0 1.2 convolution_add_fusion.8
  499.9 1.2 convolution_add_fusion.8
  504.8 1.2 convolution_add_fusion.8
  509.7 1.2 convolution_add_fusion.8
  514.6 1.2 convolution_add_fusion.8
  519.5 1.2 convolution_add_fusion.8
  524.4 1.2 convolution_add_fusion.8
  548.8 1.2 convolution_add_fusion.8
  555.4 35.6 %all_to_all.77 = bf16[8,64,1024]{2,1,0:T(8,128)(2,1)S(1)} all-to-all(bf16[8,64,1024]{2,1,0:T(8,128)(2,1)S(1)} %bitcast.121), channel_id=1, replica_groups=mesh['store'=64,'mp'=8] {'mp'}, dimensions={0} | all-to-all | bytes 2097152 | tf_op jit(solution)/shard_map/all_to_all | solution.py:102
  (464 shorter events, 152.2 us)
Async XLA Ops:
  0.0 113.2 %copy-start = (bf16[8,128,128]{2,1,0:T(8,128)(2,1)S(1)}, bf16[8,128,128]{2,1,0:T(8,128)(2,1)}, u32[]{:S(2)}) copy-start(bf16[8,128,128]{2,1,0:T(8,128)(2,1)} %param.19) | copy-start | bytes 786436
  1.6 19.4 %all-to-all-start.1 = ((bf16[64,8,128]{2,0,1:T(8,128)(2,1)}), bf16[64,8,128]{2,0,1:T(8,128)(2,1)S(1)}, u32[]{:S(2)}, u32[]{:S(2)}) async-start(bf16[64,8,128]{2,0,1:T(8,128)(2,1)} %copy_bitcast_fusion.2), calls=%async_computation.1 | async-start | bytes 262144 | tf_op jit(solution)/shard_map/all_to_all | solution.py:59
  21.0 12.4 %all-to-all-start.2 = ((bf16[64,8,128]{2,0,1:T(8,128)(2,1)}), bf16[64,8,128]{2,0,1:T(8,128)(2,1)S(1)}, u32[]{:S(2)}, u32[]{:S(2)}) async-start(bf16[64,8,128]{2,0,1:T(8,128)(2,1)} %copy_bitcast_fusion.1), calls=%async_computation.2 | async-start | bytes 262144 | tf_op jit(solution)/shard_map/all_to_all | solution.py:60
  24.4 12.6 %copy-start.7 = (s32[4,16]{1,0:T(4,128)S(1)}, s32[4,16]{1,0:T(4,128)}, u32[]{:S(2)}) copy-start(s32[4,16]{1,0:T(4,128)} %param.21) | copy-start | bytes 772
  24.4 62.6 %copy-start.1 = (s32[512]{0:T(512)S(1)}, s32[512]{0:T(512)}, u32[]{:S(2)}) copy-start(s32[512]{0:T(512)} %param.20) | copy-start | bytes 6148
  33.4 81.9 %all-to-all-start = ((bf16[64,8,1024]{2,0,1:T(8,128)(2,1)}), bf16[64,8,1024]{2,0,1:T(8,128)(2,1)S(1)}, u32[]{:S(2)}, u32[]{:S(2)}) async-start(bf16[64,8,1024]{2,0,1:T(8,128)(2,1)} %bitcast.87), calls=%async_computation | async-start | bytes 2097152 | tf_op jit(solution)/shard_map/all_to_all | solution.py:58
  115.3 8.7 %copy-start.2 = (bf16[8,128,128]{2,1,0:T(8,128)(2,1)S(1)}, bf16[8,128,128]{2,1,0:T(8,128)(2,1)}, u32[]{:S(2)}) copy-start(bf16[8,128,128]{2,1,0:T(8,128)(2,1)} %param.18) | copy-start | bytes 786436
  115.3 59.0 %all-to-all-start.4 = ((bf16[64,128,128]{2,1,0:T(8,128)(2,1)}), bf16[64,128,128]{2,1,0:T(8,128)(2,1)}, u32[]{:S(2)}, u32[]{:S(2)}) async-start(bf16[64,128,128]{2,1,0:T(8,128)(2,1)} %gather_fusion.3), calls=%async_computation.4 | async-start | bytes 4194304 | tf_op jit(solution)/shard_map/all_to_all | solution.py:82
  174.3 56.8 %all-to-all-start.3 = ((bf16[64,128,128]{2,1,0:T(8,128)(2,1)}), bf16[64,128,128]{2,1,0:T(8,128)(2,1)}, u32[]{:S(2)}, u32[]{:S(2)}) async-start(bf16[64,128,128]{2,1,0:T(8,128)(2,1)} %gather_fusion.2), calls=%async_computation.3 | async-start | bytes 4194304 | tf_op jit(solution)/shard_map/all_to_all | solution.py:81
  183.6 0.8 copy-start.6
  183.6 1.0 copy-start.5
  183.8 1.2 copy-start.4
  184.7 0.9 copy-start.3
where the time goes:
time: 603 us; the launch traced here: 592 us
  matrix products  143 us (24%)
  loops' own time  128 us (21%)
  waiting for transfers between devices  107 us (18%)
  local copies, waits for them, and re-layouts  88.2 us (15%)
  blocking collectives  85.5 us (14%)
  starting transfers between devices  32.4 us (5%)
  other arithmetic  8.39 us (1%)
    another operation x4, loops' own time, attend_head(): final, unused = lax.scan(absorb, (start_max, start_total, start_sum), order)  128 us
    dot_general x64, matrix products, absorb(): jnp.dot(weights.astype(jnp.bfloat16), block_values, preferred_element_typ...  76.6 us
    dot_general x64, matrix products, absorb(): jnp.dot(query_rows, block_keys.T, preferred_element_type=jnp.float32)  64 us
    all_gather x1, blocking collectives, local(): all_lists = lax.all_gather(retrieved, 'store', axis=0, tiled=True)  49.8 us
    all_to_all x1, waiting for transfers between devices, local(): lax.all_to_all(send_values, 'store', split_axis=0, concat_axis=0, tiled=T...  48.2 us
    dynamic_slice x64, local copies, waits for them, and re-layouts, attend_head(): final, unused = lax.scan(absorb, (start_max, start_total, start_sum), order)  47.3 us
    all_to_all x1, waiting for transfers between devices, local(): lax.all_to_all(send_keys, 'store', split_axis=0, concat_axis=0, tiled=True)  44.3 us
    all_to_all x1, blocking collectives, local(): return lax.all_to_all(result, 'mp', split_axis=0, concat_axis=1, tiled=True)  35.6 us
  transfers between devices with their start and end apart: 5, of which 4 were waited for; matrix products, arithmetic and copies ran while one was open for 7% of the time, Pallas kernels for 0%

commit v1 on v0

--- a/solution.py
+++ b/solution.py
@@ -66,7 +66,9 @@
     topc_count = retrieved.shape[1]
     rows_mine = storage_row[retrieved.reshape(-1)]
     owner_mine = rows_mine // held
-    all_lists = lax.all_gather(retrieved, "store", axis=0, tiled=True)
+    all_lists = jnp.concatenate(
+        lax.all_to_all(jnp.stack([retrieved] * lax.axis_size("store")), "store", 0, 0), axis=0
+    )
     all_rows = storage_row[all_lists.reshape(store_count, request_count * topc_count)]
     matched = all_rows // held == own_index
     wanted = jnp.sum(jnp.where(matched, all_rows % held + 1, 0), axis=1) - 1

time: 603 us -> 572 us (0.949)
  blocking collectives: 85.5 us -> 35.7 us
  waiting for transfers between devices: 107 us -> 117 us
  starting transfers between devices: 32.4 us -> 40.7 us
    all_gather x1 -> x0, blocking collectives: 49.8 us -> none  [local(): all_lists = lax.all_gather(retrieved, 'store', axis=0, tiled=True)]
    all_to_all x0 -> x1, starting transfers between devices: none -> 10.6 us  [local(): lax.all_to_all(jnp.stack([retrieved] * lax.axis_size('store')), 'store',...]
    all_to_all x0 -> x1, waiting for transfers between devices: none -> 8.59 us  [local(): lax.all_to_all(jnp.stack([retrieved] * lax.axis_size('store')), 'store',...]
  transfers between devices with their start and end apart: 5 -> 6, of which waited for: 4 -> 5; matrix products, arithmetic and copies ran while one was open for 7% -> 7% of each run, Pallas kernels for 0% -> 0%
where the time goes in v1:
time: 572 us; the launch traced here: 561 us
  matrix products  143 us (25%)
  loops' own time  128 us (22%)
  waiting for transfers between devices  117 us (20%)
  local copies, waits for them, and re-layouts  88.3 us (15%)
  starting transfers between devices  40.7 us (7%)
  blocking collectives  35.7 us (6%)
  other arithmetic  8.39 us (1%)
    another operation x4, loops' own time, attend_head(): final, unused = lax.scan(absorb, (start_max, start_total, start_sum), order)  128 us
    dot_general x64, matrix products, absorb(): jnp.dot(weights.astype(jnp.bfloat16), block_values, preferred_element_typ...  76.6 us
    dot_general x64, matrix products, absorb(): jnp.dot(query_rows, block_keys.T, preferred_element_type=jnp.float32)  64 us
    all_to_all x1, waiting for transfers between devices, local(): lax.all_to_all(send_values, 'store', split_axis=0, concat_axis=0, tiled=T...  48.2 us
    dynamic_slice x64, local copies, waits for them, and re-layouts, attend_head(): final, unused = lax.scan(absorb, (start_max, start_total, start_sum), order)  47.3 us
    all_to_all x1, waiting for transfers between devices, local(): lax.all_to_all(send_keys, 'store', split_axis=0, concat_axis=0, tiled=True)  44.3 us
    all_to_all x1, blocking collectives, local(): return lax.all_to_all(result, 'mp', split_axis=0, concat_axis=1, tiled=True)  35.7 us
    gather x2, local copies, waits for them, and re-layouts, local(): storage_row[all_lists.reshape(store_count, request_count * topc_count)]  26 us
  transfers between devices with their start and end apart: 6, of which 5 were waited for; matrix products, arithmetic and copies ran while one was open for 7% of the time, Pallas kernels for 0%

profile of v1, /device:TPU:8, one launch (start us, length us, event | category | flops | bytes accessed | tf_op | source)
XLA Modules:
  0.0 561.0 jit_solution(8309659510445261721)
XLA Ops:
  0.0 1.4 stack.2
  1.4 10.6 %all-to-all-start.3 = ((s32[64,4,16]{2,1,0:T(4,128)}), s32[64,4,16]{2,1,0:T(4,128)S(1)}, u32[]{:S(2)}, u32[]{:S(2)}) async-start(s32[64,4,16]{2,1,0:T(4,128)} %stack.2), calls=%async_computation.3 | async-start | bytes 262144 | tf_op jit(solution)/shard_map/all_to_all | solution.py:70
  12.0 1.6 copy_bitcast_fusion.2
  13.6 8.6 %all-to-all-done.3 = s32[64,4,16]{2,1,0:T(4,128)S(1)} async-done(((s32[64,4,16]{2,1,0:T(4,128)}), s32[64,4,16]{2,1,0:T(4,128)S(1)}, u32[]{:S(2)}, u32[]{:S(2)}) %all-to-all-start.3) | async-done | bytes 16416 | tf_op jit(solution)/shard_map/all_to_all | solution.py:70
  22.2 10.3 %all-to-all-start.1 = ((bf16[64,8,128]{2,0,1:T(8,128)(2,1)}), bf16[64,8,128]{2,0,1:T(8,128)(2,1)S(1)}, u32[]{:S(2)}, u32[]{:S(2)}) async-start(bf16[64,8,128]{2,0,1:T(8,128)(2,1)} %copy_bitcast_fusion.2), calls=%async_computation.1 | async-start | bytes 262144 | tf_op jit(solution)/shard_map/all_to_all | solution.py:59
  32.5 1.6 copy_bitcast_fusion.1
  34.1 7.8 %all-to-all-done.1 = bf16[64,8,128]{2,0,1:T(8,128)(2,1)S(1)} async-done(((bf16[64,8,128]{2,0,1:T(8,128)(2,1)}), bf16[64,8,128]{2,0,1:T(8,128)(2,1)S(1)}, u32[]{:S(2)}, u32[]{:S(2)}) %all-to-all-start.1) | async-done | bytes 131104 | tf_op jit(solution)/shard_map/all_to_all | solution.py:59
  41.9 3.4 all-to-all-start.2
  46.3 7.9 %all-to-all-done.2 = bf16[64,8,128]{2,0,1:T(8,128)(2,1)S(1)} async-done(((bf16[64,8,128]{2,0,1:T(8,128)(2,1)}), bf16[64,8,128]{2,0,1:T(8,128)(2,1)S(1)}, u32[]{:S(2)}, u32[]{:S(2)}) %all-to-all-start.2) | async-done | bytes 131104 | tf_op jit(solution)/shard_map/all_to_all | solution.py:60
  54.2 3.6 all-to-all-start
  58.1 25.9 %gather_fusion.1 = s32[4096]{0:T(1024)S(1)} fusion(s32[512]{0:T(512)S(1)} %copy-done.1, s32[4096]{0:T(1024)S(1)} %broadcast_clamp_fusion), kind=kCustom, calls=%fused_computation.1 | custom fusion | bytes 49152 | tf_op jit(solution)/shard_map/gather | solution.py:72
  84.2 2.1 gather_fusion.3
  86.3 6.4 %all-to-all-start.5 = ((bf16[64,128,128]{2,1,0:T(8,128)(2,1)}), bf16[64,128,128]{2,1,0:T(8,128)(2,1)}, u32[]{:S(2)}, u32[]{:S(2)}) async-start(bf16[64,128,128]{2,1,0:T(8,128)(2,1)} %gather_fusion.3), calls=%async_computation.5 | async-start | bytes 4194304 | tf_op jit(solution)/shard_map/all_to_all | solution.py:84
  92.8 2.1 gather_fusion.2
  94.9 48.2 %all-to-all-done.5 = bf16[64,128,128]{2,1,0:T(8,128)(2,1)} async-done(((bf16[64,128,128]{2,1,0:T(8,128)(2,1)}), bf16[64,128,128]{2,1,0:T(8,128)(2,1)}, u32[]{:S(2)}, u32[]{:S(2)}) %all-to-all-start.5) | async-done | bytes 2097184 | tf_op jit(solution)/shard_map/all_to_all | solution.py:84
  143.1 6.5 %all-to-all-start.4 = ((bf16[64,128,128]{2,1,0:T(8,128)(2,1)}), bf16[64,128,128]{2,1,0:T(8,128)(2,1)}, u32[]{:S(2)}, u32[]{:S(2)}) async-start(bf16[64,128,128]{2,1,0:T(8,128)(2,1)} %gather_fusion.2), calls=%async_computation.4 | async-start | bytes 4194304 | tf_op jit(solution)/shard_map/all_to_all | solution.py:83
  155.6 44.3 %all-to-all-done.4 = bf16[64,128,128]{2,1,0:T(8,128)(2,1)} async-done(((bf16[64,128,128]{2,1,0:T(8,128)(2,1)}), bf16[64,128,128]{2,1,0:T(8,128)(2,1)}, u32[]{:S(2)}, u32[]{:S(2)}) %all-to-all-start.4) | async-done | bytes 2097184 | tf_op jit(solution)/shard_map/all_to_all | solution.py:83
  200.0 88.0 %while.59 = (s32[]{:T(128)}, f32[1024]{0:T(1024)S(1)}, f32[1024]{0:T(1024)S(1)}, f32[1024,128]{1,0:T(8,128)S(1)}, s32[16]{0:T(128)}, /*index=5*/bf16[64,128,128]...) while((s32[]{:T(128)}, f32[1024]{0:T(1024)S(1)}, ...), condition=%wide.region_24.25_spmd, body=%wide.region_21.24_spmd.sunk | while | flops 68159488 | bytes 3014827 | solution.py:46
  288.3 78.3 %while.58 = (s32[]{:T(128)}, f32[1024]{0:T(1024)S(1)}, f32[1024]{0:T(1024)S(1)}, f32[1024,128]{1,0:T(8,128)S(1)}, s32[16]{0:T(128)S(1)}, /*index=5*/bf16[64,128,...) while((s32[]{:T(128)}, f32[1024]{0:T(1024)S(1)}, ...), condition=%wide.region_18.19_spmd, body=%wide.region_15.18_spmd.sunk | while | flops 68159488 | bytes 3014827 | solution.py:46
  291.9 1.2 convolution_add_fusion.10
  296.8 1.2 convolution_add_fusion.10
  301.7 1.2 convolution_add_fusion.10
  306.6 1.2 convolution_add_fusion.10
  311.5 1.2 convolution_add_fusion.10
  316.4 1.2 convolution_add_fusion.10
  321.3 1.2 convolution_add_fusion.10
  326.2 1.2 convolution_add_fusion.10
  331.1 1.2 convolution_add_fusion.10
  336.0 1.2 convolution_add_fusion.10
  340.9 1.2 convolution_add_fusion.10
  345.8 1.2 convolution_add_fusion.10
  350.7 1.2 convolution_add_fusion.10
  355.5 1.2 convolution_add_fusion.10
  360.4 1.2 convolution_add_fusion.10
  365.3 1.2 convolution_add_fusion.10
  366.9 78.3 %while.57 = (s32[]{:T(128)}, f32[1024]{0:T(1024)S(1)}, f32[1024]{0:T(1024)S(1)}, f32[1024,128]{1,0:T(8,128)S(1)}, s32[16]{0:T(128)S(1)}, /*index=5*/bf16[64,128,...) while((s32[]{:T(128)}, f32[1024]{0:T(1024)S(1)}, ...), condition=%wide.region_12.13_spmd, body=%wide.region_9.12_spmd.sunk | while | flops 68159488 | bytes 3014827 | solution.py:46
  370.6 1.2 convolution_add_fusion.9
  375.5 1.2 convolution_add_fusion.9
  380.4 1.2 convolution_add_fusion.9
  385.2 1.2 convolution_add_fusion.9
  390.1 1.2 convolution_add_fusion.9
  395.0 1.2 convolution_add_fusion.9
  399.9 1.2 convolution_add_fusion.9
  404.8 1.2 convolution_add_fusion.9
  409.7 1.2 convolution_add_fusion.9
  414.6 1.2 convolution_add_fusion.9
  419.5 1.2 convolution_add_fusion.9
  424.4 1.2 convolution_add_fusion.9
  429.3 1.2 convolution_add_fusion.9
  434.2 1.2 convolution_add_fusion.9
  439.1 1.2 convolution_add_fusion.9
  444.0 1.2 convolution_add_fusion.9
  445.5 78.3 %while.56 = (s32[]{:T(128)}, f32[1024]{0:T(1024)S(1)}, f32[1024]{0:T(1024)S(1)}, f32[1024,128]{1,0:T(8,128)S(1)}, s32[16]{0:T(128)S(1)}, /*index=5*/bf16[64,128,...) while((s32[]{:T(128)}, f32[1024]{0:T(1024)S(1)}, ...), condition=%wide.region_6.7_spmd, body=%wide.region_3.6_spmd.sunk | while | flops 68159488 | bytes 3014827 | solution.py:46
  449.2 1.2 convolution_add_fusion.8
  454.1 1.2 convolution_add_fusion.8
  459.0 1.2 convolution_add_fusion.8
  463.9 1.2 convolution_add_fusion.8
  468.8 1.2 convolution_add_fusion.8
  473.7 1.2 convolution_add_fusion.8
  478.6 1.2 convolution_add_fusion.8
  483.4 1.2 convolution_add_fusion.8
  488.3 1.2 convolution_add_fusion.8
  493.2 1.2 convolution_add_fusion.8
  524.2 35.7 %all_to_all.82 = bf16[8,64,1024]{2,1,0:T(8,128)(2,1)S(1)} all-to-all(bf16[8,64,1024]{2,1,0:T(8,128)(2,1)S(1)} %bitcast.120), channel_id=1, replica_groups=mesh['store'=64,'mp'=8] {'mp'}, dimensions={0} | all-to-all | bytes 2097152 | tf_op jit(solution)/shard_map/all_to_all | solution.py:104
  (468 shorter events, 154.4 us)
Async XLA Ops:
  0.0 84.2 %copy-start = (bf16[8,128,128]{2,1,0:T(8,128)(2,1)S(1)}, bf16[8,128,128]{2,1,0:T(8,128)(2,1)}, u32[]{:S(2)}) copy-start(bf16[8,128,128]{2,1,0:T(8,128)(2,1)} %param.19) | copy-start | bytes 786436
  0.0 45.2 %copy-start.3 = (bf16[64,8192]{1,0:T(8,128)(2,1)S(1)}, bf16[64,8192]{1,0:T(8,128)(2,1)}, u32[]{:S(2)}) copy-start(bf16[64,8192]{1,0:T(8,128)(2,1)} %param.15) | copy-start | bytes 3145732
  1.4 20.8 %all-to-all-start.3 = ((s32[64,4,16]{2,1,0:T(4,128)}), s32[64,4,16]{2,1,0:T(4,128)S(1)}, u32[]{:S(2)}, u32[]{:S(2)}) async-start(s32[64,4,16]{2,1,0:T(4,128)} %stack.2), calls=%async_computation.3 | async-start | bytes 262144 | tf_op jit(solution)/shard_map/all_to_all | solution.py:70
  22.2 19.7 %all-to-all-start.1 = ((bf16[64,8,128]{2,0,1:T(8,128)(2,1)}), bf16[64,8,128]{2,0,1:T(8,128)(2,1)S(1)}, u32[]{:S(2)}, u32[]{:S(2)}) async-start(bf16[64,8,128]{2,0,1:T(8,128)(2,1)} %copy_bitcast_fusion.2), calls=%async_computation.1 | async-start | bytes 262144 | tf_op jit(solution)/shard_map/all_to_all | solution.py:59
  41.9 12.4 %all-to-all-start.2 = ((bf16[64,8,128]{2,0,1:T(8,128)(2,1)}), bf16[64,8,128]{2,0,1:T(8,128)(2,1)S(1)}, u32[]{:S(2)}, u32[]{:S(2)}) async-start(bf16[64,8,128]{2,0,1:T(8,128)(2,1)} %copy_bitcast_fusion.1), calls=%async_computation.2 | async-start | bytes 262144 | tf_op jit(solution)/shard_map/all_to_all | solution.py:60
  45.2 12.8 %copy-start.1 = (s32[512]{0:T(512)S(1)}, s32[512]{0:T(512)}, u32[]{:S(2)}) copy-start(s32[512]{0:T(512)} %param.20) | copy-start | bytes 6148
  54.2 32.1 %all-to-all-start = ((bf16[64,8,1024]{2,0,1:T(8,128)(2,1)}), bf16[64,8,1024]{2,0,1:T(8,128)(2,1)S(1)}, u32[]{:S(2)}, u32[]{:S(2)}) async-start(bf16[64,8,1024]{2,0,1:T(8,128)(2,1)} %bitcast.86), calls=%async_computation | async-start | bytes 2097152 | tf_op jit(solution)/shard_map/all_to_all | solution.py:58
  86.3 6.4 %copy-start.2 = (bf16[8,128,128]{2,1,0:T(8,128)(2,1)S(1)}, bf16[8,128,128]{2,1,0:T(8,128)(2,1)}, u32[]{:S(2)}) copy-start(bf16[8,128,128]{2,1,0:T(8,128)(2,1)} %param.18) | copy-start | bytes 786436
  86.3 56.8 %all-to-all-start.5 = ((bf16[64,128,128]{2,1,0:T(8,128)(2,1)}), bf16[64,128,128]{2,1,0:T(8,128)(2,1)}, u32[]{:S(2)}, u32[]{:S(2)}) async-start(bf16[64,128,128]{2,1,0:T(8,128)(2,1)} %gather_fusion.3), calls=%async_computation.5 | async-start | bytes 4194304 | tf_op jit(solution)/shard_map/all_to_all | solution.py:84
  94.9 54.7 %copy-start.8 = (s32[4,16]{1,0:T(4,128)S(1)}, s32[4,16]{1,0:T(4,128)}, u32[]{:S(2)}) copy-start(s32[4,16]{1,0:T(4,128)} %param.21) | copy-start | bytes 772
  143.1 56.8 %all-to-all-start.4 = ((bf16[64,128,128]{2,1,0:T(8,128)(2,1)}), bf16[64,128,128]{2,1,0:T(8,128)(2,1)}, u32[]{:S(2)}, u32[]{:S(2)}) async-start(bf16[64,128,128]{2,1,0:T(8,128)(2,1)} %gather_fusion.2), calls=%async_computation.4 | async-start | bytes 4194304 | tf_op jit(solution)/shard_map/all_to_all | solution.py:83
  152.5 0.8 copy-start.7
  152.5 1.0 copy-start.6
  152.6 1.2 copy-start.5
  153.5 0.9 copy-start.4
